TPU v7x, 32 devices: a whole 2x2x4 slice. The times are simulated.
32 devices in a mesh: latent: 8 (over z, core), blk: 4 (over y, x).
Axes of the slice: x: 2, y: 2, z: 4, core: 2. Of those that a mesh axis runs over, the one named last changes fastest.
Arguments:
- activations: bfloat16 [4096, 8192], P(('latent', 'blk')), may hold values from -90 to 90
- block_ids: int32 [4096, 1], P(('latent', 'blk')), may hold values from 0 to 7; in each aligned block of 128 rows (0 to 127, 128 to 255, ...) at most 16 rows name the same one
- enc_weight: bfloat16 [8, 8192, 128], P('latent'), may hold values from -0.0625 to 0.0625
- enc_bias: float32 [8, 128], P('latent'), may hold values from -3 to 3
- dec_weight: bfloat16 [8, 128, 8192], P('latent'), may hold values from -0.5 to 0.5
- dec_bias: float32 [8192], replicated, may hold values from -5 to 5
Outputs:
- recon_loss: float32 [], replicated
- latent_codes: bfloat16 [4096, 128], P(('latent', 'blk'))
- dec_weight_grad: float32 [8, 128, 8192], P('latent', None, 'blk')
Inputs may be any that keep to these rules, and one draw needn't show every extreme that they name: `block_ids`: among the rows of one device, every block number is named by exactly 16 rows.
All inputs are finite; a program needn't handle non-finite values.
Results may differ from a plain program's by a relative error of at most 0.0095.
Values may be sent and summed in bfloat16 or wider, within the bound.
A program may use at most 64 MiB of HBM per device.

v0:
```python
import jax
import jax.numpy as jnp
from jax import lax
from jax.sharding import PartitionSpec as P


def local(activations, block_ids, enc_weight, enc_bias, dec_weight, dec_bias):
    groups = lax.axis_size("latent")
    replicas = lax.axis_size("blk")
    tok_rows = activations.shape[0]
    features = activations.shape[1]
    per_owner = tok_rows // groups
    block_of = block_ids[:, 0]
    matches = (block_of[:, None] == block_of[None, :]).astype(jnp.int32)
    earlier = jnp.sum(jnp.tril(matches, -1), axis=1)
    placed = block_of * per_owner + earlier
    source_row = (
        jnp.zeros((tok_rows,), jnp.int32).at[placed].set(jnp.arange(tok_rows, dtype=jnp.int32))
    )
    outgoing = activations[source_row]
    rows_block = tok_rows * replicas
    contract = (((0,), (0,)), ((), ()))
    incoming = lax.all_to_all(outgoing, "latent", split_axis=0, concat_axis=0, tiled=True)
    centered = (incoming.astype(jnp.float32) - dec_bias).astype(jnp.bfloat16)
    pre_codes = jnp.dot(centered, enc_weight[0], preferred_element_type=jnp.float32) + enc_bias[0]
    codes = jnp.maximum(pre_codes, 0.0).astype(jnp.bfloat16)
    error_rows = (
        jnp.dot(codes, dec_weight[0], preferred_element_type=jnp.float32)
        + dec_bias
        - incoming.astype(jnp.float32)
    )
    squares = jnp.sum(error_rows * error_rows)
    partial_grad = lax.dot_general(
        codes, error_rows.astype(jnp.bfloat16), contract, preferred_element_type=jnp.float32
    )
    summed = lax.psum_scatter(
        partial_grad.astype(jnp.bfloat16), "blk", scatter_dimension=1, tiled=True
    ).astype(jnp.float32)
    returned = lax.all_to_all(codes, "latent", split_axis=0, concat_axis=0, tiled=True)
    token_codes = returned[placed]
    gradient = summed / rows_block
    summed_loss = lax.psum(squares, ("latent", "blk"))
    loss_value = summed_loss / (tok_rows * groups * replicas * features)
    return (loss_value, token_codes, gradient[None])


def solution(mesh):
    placed = (
        P(("latent", "blk"), None),
        P(("latent", "blk"), None),
        P("latent", None, None),
        P("latent", None),
        P("latent", None, None),
        P(),
    )
    return jax.shard_map(
        local,
        mesh=mesh,
        in_specs=placed,
        out_specs=(P(), P(("latent", "blk"), None), P("latent", None, "blk")),
        check_vma=False,
    )
```

profile of v0, /device:TPU:0, one launch (start us, length us, event | category | flops | bytes accessed | tf_op | source)
XLA Modules:
  0.0 137.4 jit_solution(13768850276373228676)
XLA Ops:
  7.2 0.0 copy-start
  7.2 0.0 reduce-scatter.2.cloned.1.call-start
  7.2 1.0 select_reduce_fusion
  8.2 0.7 fusion.14
  8.9 1.0 scatter_custom_fusion
  9.9 7.0 %gather_fusion = bf16[128,8192]{1,0:T(8,128)(2,1)} fusion(bf16[128,8192]{1,0:T(8,128)(2,1)} %param.6, s32[1024]{0:T(1024)S(1)} %pad_clamp_fusion.1), kind=kCustom, calls=%fused_computation | custom fusion | bytes 4194816 | tf_op jit(solution)/shard_map/gather | solution.py:20
  16.9 0.0 copy-start.2
  16.9 55.5 %all_to_all.21 = bf16[8,16,8192]{2,1,0:T(8,128)(2,1)S(1)} all-to-all(bf16[8,16,8192]{2,1,0:T(8,128)(2,1)} %bitcast.36), channel_id=1, replica_groups=mesh['latent'=8,'blk'=4] {'latent'}, dimensions={0} | all-to-all | bytes 4194304 | tf_op jit(solution)/shard_map/all_to_all | solution.py:23
  72.4 0.0 copy-done.2
  72.4 0.0 copy-start.1
  72.4 0.0 copy-start.3
  72.4 0.4 subtract_convert_fusion
  72.8 1.2 copy-done.1
  74.0 0.0 copy-done.3
  74.0 1.3 fusion.11
  75.3 0.0 copy-done
  75.3 2.6 %multiply_reduce_fusion = (f32[]{:T(128)}, bf16[128,8192]{1,0:T(8,128)(2,1)S(1)}) fusion(f32[8192]{0:T(1024)S(1)} %copy-done.2, bf16[128,128]{1,0:T(8,128)(2,1)} %fusion.11, bf16[1,128,8192]{2,1,0:T(8,128)(2,1)S(1)} %copy-done, bf16[128,8192]{1,0:T(8,128)(2,1)S(1)} %bitcast.34), kind=kOutput, calls=%fused_computation.6 | convolution fusion | flops 274726912 | bytes 6356996 | tf_op jit(solution)/shard_map/dot_general | solution.py:28
  78.0 2.8 %convolution_convert_fusion = bf16[128,8192]{1,0:T(8,128)(2,1)} fusion(bf16[128,128]{1,0:T(8,128)(2,1)} %fusion.11, bf16[128,8192]{1,0:T(8,128)(2,1)S(1)} %get-tuple-element.4), kind=kOutput, calls=%fused_computation.5 | convolution fusion | flops 269484032 | bytes 4227072 | tf_op jit(solution)/shard_map/dot_general | solution.py:33
  80.8 0.0 reduce-scatter.2.cloned.1.call-update
  80.8 3.4 %all-to-all-start.1 = ((bf16[8,16,128]{2,1,0:T(8,128)(2,1)}), bf16[8,16,128]{2,1,0:T(8,128)(2,1)S(1)}, u32[]{:S(2)}, u32[]{:S(2)}) async-start(bf16[8,16,128]{2,1,0:T(8,128)(2,1)} %bitcast.9), calls=%async_computation.1 | async-start | bytes 65536 | tf_op jit(solution)/shard_map/all_to_all | solution.py:39
  84.2 41.1 %psum.7 = f32[]{:T(128)} all-reduce(f32[]{:T(128)} %get-tuple-element.3), channel_id=1, replica_groups=mesh['latent'=8,'blk'=4] {'latent','blk'}, use_global_device_ids=true, to_apply=%region_3.4 | all-reduce | flops 1 | bytes 8 | tf_op jit(solution)/shard_map/psum | solution.py:42
  126.0 0.0 all-to-all-done.1
  126.0 1.3 gather_fusion.1
  127.3 2.1 %multiply_bitcast_fusion = f32[1,128,2048]{2,1,0:T(8,128)} fusion(bf16[128,2048]{1,0:T(8,128)(2,1)} %reduce-scatter.2.cloned.1.call-done), kind=kLoop, calls=%fused_computation.15 | loop fusion | flops 524288 | bytes 1572864 | tf_op jit(solution)/shard_map/broadcast_in_dim | solution.py:44
  (6 shorter events, 0.0 us)
Async XLA Ops:
  7.2 68.2 %copy-start = (bf16[1,128,8192]{2,1,0:T(8,128)(2,1)S(1)}, bf16[1,128,8192]{2,1,0:T(8,128)(2,1)}, u32[]{:S(2)}) copy-start(bf16[1,128,8192]{2,1,0:T(8,128)(2,1)} %param.10) | copy-start | bytes 6291460
  7.2 120.1 %reduce-scatter.2.cloned.1.call-start = ((), (), s32[]{:S(2)}) async-start(), calls=%async_computation.3 | async-start | bytes 2621440 | tf_op jit(solution)/shard_map/reduce_scatter | solution.py:36
  16.9 55.5 %copy-start.2 = (f32[8192]{0:T(1024)S(1)}, f32[8192]{0:T(1024)}, u32[]{:S(2)}) copy-start(f32[8192]{0:T(1024)} %param.11) | copy-start | bytes 98308
  72.4 1.6 %copy-start.1 = (bf16[1,8192,128]{2,1,0:T(8,128)(2,1)S(1)}, bf16[1,8192,128]{2,1,0:T(8,128)(2,1)}, u32[]{:S(2)}) copy-start(bf16[1,8192,128]{2,1,0:T(8,128)(2,1)} %param.8) | copy-start | bytes 6291460
  72.4 1.6 %copy-start.3 = (f32[1,128]{1,0:T(1,128)S(1)}, f32[1,128]{1,0:T(1,128)}, u32[]{:S(2)}) copy-start(f32[1,128]{1,0:T(1,128)} %param.9) | copy-start | bytes 1540
  80.8 45.2 %all-to-all-start.1 = ((bf16[8,16,128]{2,1,0:T(8,128)(2,1)}), bf16[8,16,128]{2,1,0:T(8,128)(2,1)S(1)}, u32[]{:S(2)}, u32[]{:S(2)}) async-start(bf16[8,16,128]{2,1,0:T(8,128)(2,1)} %bitcast.9), calls=%async_computation.1 | async-start | bytes 65536 | tf_op jit(solution)/shard_map/all_to_all | solution.py:39
Sparse Core Ops, SparseCore 0:
  80.9 34.8 reduce-scatter.1
where the time goes:
time: 138 us; the launch traced here: 137 us
  blocking collectives  96.7 us (70%)
  between operations  15.9 us (12%)
  local copies, waits for them, and re-layouts  10.5 us (8%)
  matrix products  6.8 us (5%)
  other arithmetic  4.2 us (3%)
  starting transfers between devices  3.39 us (2%)
    all_to_all x1, blocking collectives, local(): lax.all_to_all(outgoing, 'latent', split_axis=0, concat_axis=0, tiled=True)  55.5 us
    psum x1, blocking collectives, local(): summed_loss = lax.psum(squares, ('latent', 'blk'))  41.1 us
    gather x1, local copies, waits for them, and re-layouts, local(): outgoing = activations[source_row]  6.98 us
    all_to_all x1, starting transfers between devices, local(): lax.all_to_all(codes, 'latent', split_axis=0, concat_axis=0, tiled=True)  3.35 us
    dot_general x1, matrix products, local(): lax.dot_general(codes, error_rows.astype(jnp.bfloat16), contract, preferr...  2.85 us
  transfers between devices with their start and end apart: 2, of which 0 were waited for; matrix products, arithmetic and copies ran while one was open for 1% of the time, Pallas kernels for 0%

commit v1 on v0

--- a/solution.py
+++ b/solution.py
@@ -1,14 +1,343 @@
+import functools
+
 import jax
 import jax.numpy as jnp
 from jax import lax
+from jax.experimental import pallas as pl
+from jax.experimental.pallas import tpu as pltpu
 from jax.sharding import PartitionSpec as P
 
-
-def local(activations, block_ids, enc_weight, enc_bias, dec_weight, dec_bias):
+MESH = pl.DeviceIdType.MESH
+
+
+def flip(index, mask):
+    out, bit = index, 1
+    while bit <= mask:
+        if mask & bit:
+            out = out + bit * (1 - 2 * ((index // bit) % 2))
+        bit *= 2
+    return out
+
+
+def kernel(
+    groups,
+    replicas,
+    tile,
+    ids_ref,
+    enc_bias_ref,
+    dec_bias_ref,
+    act_hbm,
+    enc_hbm,
+    dec_hbm,
+    loss_ref,
+    codes_out_ref,
+    grad_ref,
+    act,
+    ordered,
+    arrived,
+    enc,
+    dec,
+    parts,
+    codes,
+    returned,
+    squares,
+    losses,
+    load_sem,
+    row_send,
+    row_recv,
+    part_send,
+    part_recv,
+    code_send,
+    code_recv,
+    loss_send,
+    loss_recv,
+):
+    lat, blk = lax.axis_index("latent"), lax.axis_index("blk")
+    tok_rows, features = act.shape
+    seg = tok_rows // groups
+    width = features // replicas
+    latents = enc.shape[1]
+    tiles = width // tile
+    group_rows = 2 * replicas * seg
+    own_cols = pl.multiple_of(blk * width, width)
+    pairs = [(groups // 2 + i, groups // 2 - 1 - i) for i in range(groups // 2)]
+    peers = [(j, e) for j in range(groups) for e in range(replicas) if (j, e) != (0, 0)]
+
+    def device(j, e):
+        return (flip(lat, j), flip(blk, e))
+
+    barrier = pltpu.get_barrier_semaphore()
+    loads = []
+    for e in range(replicas):
+        cols = pl.ds(pl.multiple_of(flip(blk, e) * width, width), width)
+        loads.append(
+            pltpu.make_async_copy(act_hbm.at[:, cols], act.at[:, cols], load_sem.at[e])
+        )
+    load_enc = pltpu.make_async_copy(
+        enc_hbm.at[0, pl.ds(own_cols, width), :], enc, load_sem.at[replicas]
+    )
+    load_dec = pltpu.make_async_copy(
+        dec_hbm.at[0, :, pl.ds(own_cols, width)], dec, load_sem.at[replicas + 1]
+    )
+    for load in loads:
+        load.start()
+    for j, e in peers:
+        pl.semaphore_signal(barrier, inc=1, device_id=device(j, e), device_id_type=MESH)
+    load_enc.start()
+    load_dec.start()
+
+    ids = ids_ref[...]
+    named = ids == lax.broadcasted_iota(jnp.int32, (tok_rows, 128), 1)
+    lower = lax.broadcasted_iota(jnp.int32, (tok_rows, tok_rows), 0) > lax.broadcasted_iota(
+        jnp.int32, (tok_rows, tok_rows), 1
+    )
+    named_f = named.astype(jnp.float32)
+    earlier = jnp.dot(
+        lower.astype(jnp.float32).astype(jnp.bfloat16),
+        named_f.astype(jnp.bfloat16),
+        preferred_element_type=jnp.float32,
+    )
+    place = jnp.sum(named_f * earlier, axis=1, keepdims=True) + ids.astype(jnp.float32) * seg
+    spot = lax.broadcasted_iota(jnp.int32, (tok_rows, tok_rows), 1).astype(jnp.float32)
+    to_token = (place == spot).astype(jnp.float32)
+    to_place = to_token.T.astype(jnp.bfloat16)
+
+    for e in range(replicas):
+        loads[e].wait()
+
+        def order_rows(i, carry):
+            cols = pl.ds(pl.multiple_of(flip(blk, e) * width + i * tile, tile), tile)
+            ordered[:, cols] = jnp.dot(
+                to_place, act[:, cols], preferred_element_type=jnp.float32
+            ).astype(jnp.bfloat16)
+            return carry
+
+        lax.fori_loop(0, tiles, order_rows, 0)
+
+    pl.semaphore_wait(barrier, len(peers))
+
+    row_copies = {}
+    for pair_at, pair in enumerate(pairs):
+        for e in range(replicas):
+            for side, j in enumerate(pair):
+                owner, column = device(j, e)
+                source = ordered.at[
+                    pl.ds(pl.multiple_of(owner * seg, seg), seg),
+                    pl.ds(pl.multiple_of(column * width, width), width),
+                ]
+                slot = (2 * pair_at + side) * replicas + blk
+                target = arrived.at[pl.ds(pl.multiple_of(slot * seg, seg), seg), :]
+                if (j, e) == (0, 0):
+                    copy = pltpu.make_async_copy(source, target, row_recv.at[0])
+                else:
+                    copy = pltpu.make_async_remote_copy(
+                        src_ref=source,
+                        dst_ref=target,
+                        send_sem=row_send.at[j * replicas + e],
+                        recv_sem=row_recv.at[j * replicas + e],
+                        device_id=(owner, column),
+                        device_id_type=MESH,
+                    )
+                copy.start()
+                row_copies[j, e] = copy
+
+    load_enc.wait()
+    load_dec.wait()
+    squares[...] = jnp.zeros_like(squares)
+    part_copies, code_copies = [], []
+
+    def encode(pair_at):
+        for e in range(replicas):
+            for j in pairs[pair_at]:
+                if (j, e) == (0, 0):
+                    row_copies[j, e].wait()
+                else:
+                    row_copies[j, e].wait_recv()
+
+        def step(i, total):
+            cols = pl.ds(pl.multiple_of(i * tile, tile), tile)
+            bias = dec_bias_ref[:, pl.ds(pl.multiple_of(own_cols + i * tile, tile), tile)]
+            rows = arrived[pl.ds(pair_at * group_rows, group_rows), cols]
+            centered = (rows.astype(jnp.float32) - bias).astype(jnp.bfloat16)
+            return total + jnp.dot(centered, enc[cols, :], preferred_element_type=jnp.float32)
+
+        parts[pair_at, blk] = lax.fori_loop(
+            0, tiles, step, jnp.zeros((group_rows, latents), jnp.float32)
+        )
+        for e in range(1, replicas):
+            copy = pltpu.make_async_remote_copy(
+                src_ref=parts.at[pair_at, blk],
+                dst_ref=parts.at[pair_at, blk],
+                send_sem=part_send.at[pair_at * replicas + e],
+                recv_sem=part_recv.at[pair_at * replicas + e],
+                device_id=device(0, e),
+                device_id_type=MESH,
+            )
+            copy.start()
+            part_copies.append(copy)
+
+    def decode(pair_at):
+        for copy in part_copies[pair_at * (replicas - 1) : (pair_at + 1) * (replicas - 1)]:
+            copy.wait_recv()
+        total = parts[pair_at, 0]
+        for d in range(1, replicas):
+            total = total + parts[pair_at, d]
+        wide = jnp.maximum(total + enc_bias_ref[...], 0.0)
+        low = wide.astype(jnp.bfloat16)
+        flipped = low.astype(jnp.float32).T.astype(jnp.bfloat16)
+        codes[pl.ds(pair_at * group_rows, group_rows), :] = low
+        home = pl.ds(pl.multiple_of(lat * seg, seg), seg)
+        for side, j in enumerate(pairs[pair_at]):
+            slot = (2 * pair_at + side) * replicas + blk
+            source = codes.at[pl.ds(pl.multiple_of(slot * seg, seg), seg), :]
+            if j == 0:
+                copy = pltpu.make_async_copy(source, returned.at[home, :], code_recv.at[0])
+            else:
+                copy = pltpu.make_async_remote_copy(
+                    src_ref=source,
+                    dst_ref=returned.at[home, :],
+                    send_sem=code_send.at[j],
+                    recv_sem=code_recv.at[j],
+                    device_id=device(j, 0),
+                    device_id_type=MESH,
+                )
+            copy.start()
+            code_copies.append((j, copy))
+
+        def step(i, carry):
+            cols = pl.ds(pl.multiple_of(i * tile, tile), tile)
+            bias = dec_bias_ref[:, pl.ds(pl.multiple_of(own_cols + i * tile, tile), tile)]
+            rows = arrived[pl.ds(pair_at * group_rows, group_rows), cols]
+            error = (
+                jnp.dot(low, dec[:, cols], preferred_element_type=jnp.float32)
+                + bias
+                - rows.astype(jnp.float32)
+            )
+            squares[:, cols] += jnp.sum(
+                (error * error).reshape(group_rows // 8, 8, tile), axis=0
+            )
+            term = jnp.dot(
+                flipped, error.astype(jnp.bfloat16), preferred_element_type=jnp.float32
+            )
+            if pair_at > 0:
+                term = grad_ref[0, :, cols] + term
+            if pair_at == len(pairs) - 1:
+                term = term / (tok_rows * replicas)
+            grad_ref[0, :, cols] = term
+            return carry
+
+        lax.fori_loop(0, tiles, step, 0)
+
+    for pair_at in range(len(pairs)):
+        encode(pair_at)
+        if pair_at > 0:
+            decode(pair_at - 1)
+    decode(len(pairs) - 1)
+
+    own = squares[:, :128]
+    for i in range(1, width // 128):
+        own = own + squares[:, i * 128 : (i + 1) * 128]
+    place_of = lat * replicas + blk
+    losses[place_of] = own
+    loss_copies = []
+    for j, e in peers:
+        copy = pltpu.make_async_remote_copy(
+            src_ref=losses.at[place_of],
+            dst_ref=losses.at[place_of],
+            send_sem=loss_send.at[j * replicas + e],
+            recv_sem=loss_recv.at[j * replicas + e],
+            device_id=device(j, e),
+            device_id_type=MESH,
+        )
+        copy.start()
+        loss_copies.append(copy)
+
+    for j, copy in code_copies:
+        if j == 0:
+            copy.wait()
+        else:
+            copy.wait_recv()
+    codes_out_ref[...] = jnp.dot(
+        to_token.astype(jnp.bfloat16), returned[...], preferred_element_type=jnp.float32
+    ).astype(jnp.bfloat16)
+
+    for copy in loss_copies:
+        copy.wait_recv()
+    total = jnp.sum(losses[...], axis=0)
+    loss_ref[...] = jnp.sum(total, keepdims=True) / (
+        tok_rows * groups * replicas * features
+    )
+
+    for j, e in peers:
+        row_copies[j, e].wait_send()
+    for copy in part_copies + loss_copies:
+        copy.wait_send()
+    for j, copy in code_copies:
+        if j > 0:
+            copy.wait_send()
+
+
+def routed(activations, block_ids, enc_weight, enc_bias, dec_weight, dec_bias):
     groups = lax.axis_size("latent")
     replicas = lax.axis_size("blk")
-    tok_rows = activations.shape[0]
-    features = activations.shape[1]
+    devices = groups * replicas
+    tok_rows, features = activations.shape
+    latents = enc_weight.shape[2]
+    seg = tok_rows // groups
+    width = features // replicas
+    pairs = groups // 2
+    tile = min(512, width)
+    vmem = pl.BlockSpec(memory_space=pltpu.VMEM)
+    hbm = pl.BlockSpec(memory_space=pl.ANY)
+    dma = pltpu.SemaphoreType.DMA
+    loss, codes, gradient = pl.pallas_call(
+        functools.partial(kernel, groups, replicas, tile),
+        out_shape=(
+            jax.ShapeDtypeStruct((1, 1), jnp.float32),
+            jax.ShapeDtypeStruct((tok_rows, latents), jnp.bfloat16),
+            jax.ShapeDtypeStruct((1, latents, width), jnp.float32),
+        ),
+        in_specs=[vmem, vmem, vmem, hbm, hbm, hbm],
+        out_specs=(vmem, vmem, vmem),
+        scratch_shapes=[
+            pltpu.VMEM((tok_rows, features), jnp.bfloat16),
+            pltpu.VMEM((tok_rows, features), jnp.bfloat16),
+            pltpu.VMEM((devices * seg, width), jnp.bfloat16),
+            pltpu.VMEM((width, latents), jnp.bfloat16),
+            pltpu.VMEM((latents, width), jnp.bfloat16),
+            pltpu.VMEM((pairs, replicas, 2 * replicas * seg, latents), jnp.float32),
+            pltpu.VMEM((devices * seg, latents), jnp.bfloat16),
+            pltpu.VMEM((tok_rows, latents), jnp.bfloat16),
+            pltpu.VMEM((8, width), jnp.float32),
+            pltpu.VMEM((devices, 8, 128), jnp.float32),
+            dma((replicas + 2,)),
+            dma((devices,)),
+            dma((devices,)),
+            dma((pairs * replicas,)),
+            dma((pairs * replicas,)),
+            dma((groups,)),
+            dma((groups,)),
+            dma((devices,)),
+            dma((devices,)),
+        ],
+        compiler_params=pltpu.CompilerParams(
+            collective_id=0, has_side_effects=True, vmem_limit_bytes=40 * 1024 * 1024
+        ),
+    )(
+        block_ids,
+        enc_bias,
+        dec_bias.reshape(1, features),
+        activations,
+        enc_weight,
+        dec_weight,
+    )
+    return loss[0, 0], codes, gradient
+
+
+def spread(activations, block_ids, enc_weight, enc_bias, dec_weight, dec_bias):
+    groups = lax.axis_size("latent")
+    replicas = lax.axis_size("blk")
+    tok_rows, features = activations.shape
     per_owner = tok_rows // groups
     block_of = block_ids[:, 0]
     matches = (block_of[:, None] == block_of[None, :]).astype(jnp.int32)
@@ -18,7 +347,6 @@
         jnp.zeros((tok_rows,), jnp.int32).at[placed].set(jnp.arange(tok_rows, dtype=jnp.int32))
     )
     outgoing = activations[source_row]
-    rows_block = tok_rows * replicas
     contract = (((0,), (0,)), ((), ()))
     incoming = lax.all_to_all(outgoing, "latent", split_axis=0, concat_axis=0, tiled=True)
     centered = (incoming.astype(jnp.float32) - dec_bias).astype(jnp.bfloat16)
@@ -38,13 +366,14 @@
     ).astype(jnp.float32)
     returned = lax.all_to_all(codes, "latent", split_axis=0, concat_axis=0, tiled=True)
     token_codes = returned[placed]
-    gradient = summed / rows_block
+    gradient = summed / (tok_rows * replicas)
     summed_loss = lax.psum(squares, ("latent", "blk"))
     loss_value = summed_loss / (tok_rows * groups * replicas * features)
     return (loss_value, token_codes, gradient[None])
 
 
 def solution(mesh):
+    groups, replicas = mesh.shape["latent"], mesh.shape["blk"]
     placed = (
         P(("latent", "blk"), None),
         P(("latent", "blk"), None),
@@ -53,6 +382,17 @@
         P("latent", None, None),
         P(),
     )
+
+    def local(activations, *rest):
+        tok_rows, features = activations.shape
+        fits = (
+            groups & (groups - 1) == 0
+            and replicas & (replicas - 1) == 0
+            and tok_rows % (16 * groups) == 0
+            and features % (128 * replicas) == 0
+        )
+        return (routed if fits else spread)(activations, *rest)
+
     return jax.shard_map(
         local,
         mesh=mesh,

time: 138 us -> 80 us (0.58)
  blocking collectives: 96.7 us -> 0 us
  Pallas kernels: 0 us -> 68.8 us
  between operations: 15.9 us -> 2.34 us
  matrix products: 6.8 us -> 0 us
  other arithmetic: 4.2 us -> 0 us
  starting transfers between devices: 3.39 us -> 0 us
  local copies, waits for them, and re-layouts: 10.5 us -> 8.53 us
    pallas_call x0 -> x1, Pallas kernels: none -> 68.8 us  [routed(): pl.pallas_call(functools.partial(kernel, groups, replicas, tile), out_sha...]
    all_to_all x1 -> x0, blocking collectives: 55.5 us -> none  [local(): lax.all_to_all(outgoing, 'latent', split_axis=0, concat_axis=0, tiled=True)]
    psum x1 -> x0, blocking collectives: 41.1 us -> none  [local(): summed_loss = lax.psum(squares, ('latent', 'blk'))]
    gather x2 -> x0, local copies, waits for them, and re-layouts: 8.29 us -> none  [the longest x1 6.98 us: local(): outgoing = activations[source_row]]
    unnamed x8 -> x13, local copies, waits for them, and re-layouts: 1.2 us -> 8.53 us
    dot_general x3 -> x0, matrix products: 6.8 us -> none  [the longest x1 2.85 us: local(): lax.dot_general(codes, error_rows.astype(jnp.bfloat16), contract, preferr...]
    all_to_all x1 -> x0, starting transfers between devices: 3.35 us -> none  [local(): lax.all_to_all(codes, 'latent', split_axis=0, concat_axis=0, tiled=True)]
    broadcast_in_dim x1 -> x0, other arithmetic: 2.12 us -> none  [local(): return (loss_value, token_codes, gradient[None])]
  transfers between devices with their start and end apart: 2 -> 0, of which waited for: 0 -> 0; matrix products, arithmetic and copies ran while one was open for 1% -> 0% of each run, Pallas kernels for 0% -> 0%
where the time goes in v1:
time: 80 us; the launch traced here: 79.7 us
  Pallas kernels  68.8 us (86%)
  local copies, waits for them, and re-layouts  8.53 us (11%)
  between operations  2.34 us (3%)
    pallas_call x1, Pallas kernels, routed(): pl.pallas_call(functools.partial(kernel, groups, replicas, tile), out_sha...  68.8 us
    unnamed x13, local copies, waits for them, and re-layouts  8.53 us

profile of v1, /device:TPU:0, one launch (start us, length us, event | category | flops | bytes accessed | tf_op | source)
XLA Modules:
  0.0 79.7 jit_solution(16449314296181215955)
XLA Ops:
  0.6 0.8 copy.9.ids_ref
  1.4 0.0 copy-start
  1.4 1.6 %copy-done = bf16[128,8192]{1,0:T(8,128)(2,1)S(1)} copy-done((bf16[128,8192]{1,0:T(8,128)(2,1)S(1)}, bf16[128,8192]{1,0:T(8,128)(2,1)}, u32[]{:S(2)}) %copy-start) | copy-done | bytes 2097176
  3.0 0.0 copy-start.1
  3.0 1.6 %copy-done.1 = bf16[1,8192,128]{2,1,0:T(8,128)(2,1)S(1)} copy-done((bf16[1,8192,128]{2,1,0:T(8,128)(2,1)S(1)}, bf16[1,8192,128]{2,1,0:T(8,128)(2,1)}, u32[]{:S(2)}) %copy-start.1) | copy-done | bytes 2097176
  4.6 0.0 copy-start.2
  4.6 1.6 %copy-done.2 = bf16[1,128,8192]{2,1,0:T(8,128)(2,1)S(1)} copy-done((bf16[1,128,8192]{2,1,0:T(8,128)(2,1)S(1)}, bf16[1,128,8192]{2,1,0:T(8,128)(2,1)}, u32[]{:S(2)}) %copy-start.2) | copy-done | bytes 2097176
  6.2 0.0 copy-start.3
  6.2 0.8 copy-done.3
  6.9 0.0 copy-start.4
  6.9 0.7 copy-done.4
  7.6 68.8 %shard_map.85 = (f32[1,1]{1,0:T(1,128)}, bf16[128,128]{1,0:T(8,128)(2,1)S(1)}, f32[1,128,2048]{2,1,0:T(8,128)S(1)}) custom-call(s32[128,1]{1,0:T(8,128)S(1)} %copy.9.ids_ref, f32[1,128]{1,0:T(1,128)S(1)} %copy-done.4, f32[1,8192]{1,0:T(1,128)S(1)} %bitcast.2, bf16[128,8192]{1,0:T(8,128)(2,1)S(1)} %copy-done, bf16[1,8192,128]{2,1,0:T(8,128)(2,1)S(1)} %copy-done.1, ...), custom_call_target="tpu_custom_call" | custom-call | tf_op jit(solution)/shard_map/pallas_call | solution.py:293
  77.0 0.6 copy.14
  77.6 1.0 %copy.15 = f32[1,128,2048]{2,1,0:T(8,128)} copy(f32[1,128,2048]{2,1,0:T(8,128)S(1)} %get-tuple-element.14) | data formatting | bytes 2097152
Async XLA Ops:
  1.4 1.6 %copy-start = (bf16[128,8192]{1,0:T(8,128)(2,1)S(1)}, bf16[128,8192]{1,0:T(8,128)(2,1)}, u32[]{:S(2)}) copy-start(bf16[128,8192]{1,0:T(8,128)(2,1)} %act_hbm.1) | copy-start | bytes 6291460
  3.0 1.6 %copy-start.1 = (bf16[1,8192,128]{2,1,0:T(8,128)(2,1)S(1)}, bf16[1,8192,128]{2,1,0:T(8,128)(2,1)}, u32[]{:S(2)}) copy-start(bf16[1,8192,128]{2,1,0:T(8,128)(2,1)} %enc_hbm.1) | copy-start | bytes 6291460
  4.6 1.6 %copy-start.2 = (bf16[1,128,8192]{2,1,0:T(8,128)(2,1)S(1)}, bf16[1,128,8192]{2,1,0:T(8,128)(2,1)}, u32[]{:S(2)}) copy-start(bf16[1,128,8192]{2,1,0:T(8,128)(2,1)} %dec_hbm.1) | copy-start | bytes 6291460
  6.2 0.8 copy-start.3
  6.9 0.7 copy-start.4

commit v2 on v1

v2 whole, which is shorter than its diff:
```python
import functools
import math

import jax
import jax.numpy as jnp
from jax import lax
from jax.experimental import pallas as pl
from jax.experimental.pallas import tpu as pltpu
from jax.sharding import PartitionSpec as P

MESH = pl.DeviceIdType.MESH


def flip(index, mask):
    out, bit = index, 1
    while bit <= mask:
        if mask & bit:
            out = out + bit * (1 - 2 * ((index // bit) % 2))
        bit *= 2
    return out


def kernel(
    groups,
    replicas,
    tile,
    ids_ref,
    enc_bias_ref,
    dec_bias_ref,
    act_hbm,
    enc_hbm,
    dec_hbm,
    loss_ref,
    codes_out_ref,
    grad_hbm,
    act,
    ordered,
    arrived,
    enc,
    dec,
    parts,
    codes,
    returned,
    squares,
    losses,
    error_low,
    grad,
    load_sem,
    row_send,
    row_recv,
    part_send,
    part_recv,
    code_send,
    code_recv,
    loss_send,
    loss_recv,
):
    lat, blk = lax.axis_index("latent"), lax.axis_index("blk")
    tok_rows, features = act.shape
    seg = tok_rows // groups
    width = features // replicas
    latents = enc.shape[1]
    tiles = width // tile
    group_rows = replicas * seg
    own_cols = pl.multiple_of(blk * width, width)
    order = [j for i in range(groups // 2) for j in (groups // 2 - 1 - i, groups // 2 + i)]
    ahead = min(4, groups)
    peers = [(j, e) for j in range(groups) for e in range(replicas) if (j, e) != (0, 0)]

    def device(j, e):
        return (flip(lat, j), flip(blk, e))

    barrier = pltpu.get_barrier_semaphore()
    loads = []
    for e in range(replicas):
        cols = pl.ds(pl.multiple_of(flip(blk, e) * width, width), width)
        loads.append(
            pltpu.make_async_copy(act_hbm.at[:, cols], act.at[:, cols], load_sem.at[e])
        )
    load_enc = pltpu.make_async_copy(
        enc_hbm.at[0, pl.ds(own_cols, width), :], enc, load_sem.at[replicas]
    )
    load_dec = pltpu.make_async_copy(
        dec_hbm.at[0, :, pl.ds(own_cols, width)], dec, load_sem.at[replicas + 1]
    )
    for load in loads:
        load.start()
    for j, e in peers:
        pl.semaphore_signal(barrier, inc=1, device_id=device(j, e), device_id_type=MESH)
    load_enc.start()
    load_dec.start()

    ids = ids_ref[...]
    square = (tok_rows, tok_rows)
    down = lax.broadcasted_iota(jnp.int32, square, 0)
    along = lax.broadcasted_iota(jnp.int32, square, 1)
    named = (ids == down).astype(jnp.float32)
    earlier = jnp.dot(
        named.astype(jnp.bfloat16),
        (down < along).astype(jnp.float32).astype(jnp.bfloat16),
        preferred_element_type=jnp.float32,
    )
    place = jnp.sum(named * earlier, axis=0, keepdims=True) + ids.astype(jnp.float32) * seg
    placed = (place == down.astype(jnp.float32)).astype(jnp.float32)
    to_place = placed.astype(jnp.bfloat16)

    row_copies = {}

    def send_rows(at, e):
        j = order[at]
        owner, column = device(j, e)
        source = ordered.at[
            pl.ds(pl.multiple_of(owner * seg, seg), seg),
            pl.ds(pl.multiple_of(column * width, width), width),
        ]
        target = arrived.at[pl.ds(pl.multiple_of((at * replicas + blk) * seg, seg), seg), :]
        if (j, e) == (0, 0):
            copy = pltpu.make_async_copy(source, target, row_recv.at[0])
        else:
            copy = pltpu.make_async_remote_copy(
                src_ref=source,
                dst_ref=target,
                send_sem=row_send.at[j * replicas + e],
                recv_sem=row_recv.at[j * replicas + e],
                device_id=(owner, column),
                device_id_type=MESH,
            )
        copy.start()
        row_copies[j, e] = copy

    def wait_sent(at):
        for e in range(replicas):
            if (order[at], e) != (0, 0):
                row_copies[order[at], e].wait_send()

    for e in range(replicas):
        loads[e].wait()

        def order_rows(i, carry):
            cols = pl.ds(pl.multiple_of(flip(blk, e) * width + i * tile, tile), tile)
            ordered[:, cols] = jnp.dot(
                to_place, act[:, cols], preferred_element_type=jnp.float32
            ).astype(jnp.bfloat16)
            return carry

        lax.fori_loop(0, tiles, order_rows, 0)
        if e == 0:
            pl.semaphore_wait(barrier, len(peers))
        for at in range(ahead):
            send_rows(at, e)

    load_enc.wait()
    load_dec.wait()
    squares[...] = jnp.zeros_like(squares)
    part_copies, code_copies = [], []

    def encode(at):
        for e in range(replicas):
            if (order[at], e) == (0, 0):
                row_copies[0, 0].wait()
            else:
                row_copies[order[at], e].wait_recv()

        def step(i, total):
            cols = pl.ds(pl.multiple_of(i * tile, tile), tile)
            bias = dec_bias_ref[:, pl.ds(pl.multiple_of(own_cols + i * tile, tile), tile)]
            rows = arrived[pl.ds(at * group_rows, group_rows), cols]
            centered = (rows.astype(jnp.float32) - bias).astype(jnp.bfloat16)
            return total + jnp.dot(centered, enc[cols, :], preferred_element_type=jnp.float32)

        parts[at, blk] = lax.fori_loop(
            0, tiles, step, jnp.zeros((group_rows, latents), jnp.float32)
        )
        for e in range(1, replicas):
            copy = pltpu.make_async_remote_copy(
                src_ref=parts.at[at, blk],
                dst_ref=parts.at[at, blk],
                send_sem=part_send.at[at * replicas + e],
                recv_sem=part_recv.at[at * replicas + e],
                device_id=device(0, e),
                device_id_type=MESH,
            )
            copy.start()
            part_copies.append(copy)

    def decode(at):
        for copy in part_copies[at * (replicas - 1) : (at + 1) * (replicas - 1)]:
            copy.wait_recv()
        total = parts[at, 0]
        for d in range(1, replicas):
            total = total + parts[at, d]
        wide = jnp.maximum(total + enc_bias_ref[...], 0.0)
        low = wide.astype(jnp.bfloat16)
        flipped = low.astype(jnp.float32).T.astype(jnp.bfloat16)
        codes[pl.ds(at * group_rows, group_rows), :] = low
        j = order[at]
        home = pl.ds(pl.multiple_of(lat * seg, seg), seg)
        source = codes.at[pl.ds(pl.multiple_of((at * replicas + blk) * seg, seg), seg), :]
        if j == 0:
            copy = pltpu.make_async_copy(source, returned.at[home, :], code_recv.at[0])
        else:
            copy = pltpu.make_async_remote_copy(
                src_ref=source,
                dst_ref=returned.at[home, :],
                send_sem=code_send.at[j],
                recv_sem=code_recv.at[j],
                device_id=device(j, 0),
                device_id_type=MESH,
            )
        copy.start()
        code_copies.append((j, copy))

        def errors(i, carry):
            cols = pl.ds(pl.multiple_of(i * tile, tile), tile)
            bias = dec_bias_ref[:, pl.ds(pl.multiple_of(own_cols + i * tile, tile), tile)]
            rows = arrived[pl.ds(at * group_rows, group_rows), cols]
            error = (
                jnp.dot(low, dec[:, cols], preferred_element_type=jnp.float32)
                + bias
                - rows.astype(jnp.float32)
            )
            squares[:, cols] += jnp.sum(
                (error * error).reshape(group_rows // 8, 8, tile), axis=0
            )
            error_low[:, cols] = error.astype(jnp.bfloat16)
            return carry

        def gradient(i, carry):
            cols = pl.ds(pl.multiple_of(i * tile, tile), tile)
            term = jnp.dot(flipped, error_low[:, cols], preferred_element_type=jnp.float32)
            if at > 0:
                term = grad[:, cols] + term
            if at == groups - 1:
                term = term / (tok_rows * replicas)
            grad[:, cols] = term
            return carry

        lax.fori_loop(0, tiles, errors, 0)
        if at == groups - 1:
            send_squares()
        lax.fori_loop(0, tiles, gradient, 0)

    place_of = lat * replicas + blk
    loss_copies = []

    def send_squares():
        own = squares[:, :128]
        for i in range(1, width // 128):
            own = own + squares[:, i * 128 : (i + 1) * 128]
        losses[place_of] = own
        for j, e in peers:
            copy = pltpu.make_async_remote_copy(
                src_ref=losses.at[place_of],
                dst_ref=losses.at[place_of],
                send_sem=loss_send.at[j * replicas + e],
                recv_sem=loss_recv.at[j * replicas + e],
                device_id=device(j, e),
                device_id_type=MESH,
            )
            copy.start()
            loss_copies.append(copy)

    for at in range(groups):
        if at + ahead < groups:
            wait_sent(at)
            for e in range(replicas):
                send_rows(at + ahead, e)
        encode(at)
        if at > 0:
            decode(at - 1)
    decode(groups - 1)
    store = pltpu.make_async_copy(grad, grad_hbm.at[0], load_sem.at[0])
    store.start()

    for j, copy in code_copies:
        if j == 0:
            copy.wait()
        else:
            copy.wait_recv()
    codes_out_ref[...] = jnp.dot(
        placed.T.astype(jnp.bfloat16), returned[...], preferred_element_type=jnp.float32
    ).astype(jnp.bfloat16)

    for copy in loss_copies:
        copy.wait_recv()
    total = jnp.sum(losses[...], axis=0)
    loss_ref[...] = jnp.sum(total, keepdims=True) / (
        tok_rows * groups * replicas * features
    )

    store.wait()
    for at in range(groups - ahead, groups):
        wait_sent(at)
    for copy in part_copies + loss_copies:
        copy.wait_send()
    for j, copy in code_copies:
        if j > 0:
            copy.wait_send()


def routed(activations, block_ids, enc_weight, enc_bias, dec_weight, dec_bias):
    groups = lax.axis_size("latent")
    replicas = lax.axis_size("blk")
    devices = groups * replicas
    tok_rows, features = activations.shape
    latents = enc_weight.shape[2]
    seg = tok_rows // groups
    width = features // replicas
    tile = math.gcd(512, width)
    vmem = pl.BlockSpec(memory_space=pltpu.VMEM)
    hbm = pl.BlockSpec(memory_space=pl.ANY)
    dma = pltpu.SemaphoreType.DMA
    loss, codes, gradient = pl.pallas_call(
        functools.partial(kernel, groups, replicas, tile),
        out_shape=(
            jax.ShapeDtypeStruct((1, 1), jnp.float32),
            jax.ShapeDtypeStruct((tok_rows, latents), jnp.bfloat16),
            jax.ShapeDtypeStruct((1, latents, width), jnp.float32),
        ),
        in_specs=[vmem, vmem, vmem, hbm, hbm, hbm],
        out_specs=(vmem, vmem, hbm),
        scratch_shapes=[
            pltpu.VMEM((tok_rows, features), jnp.bfloat16),
            pltpu.VMEM((tok_rows, features), jnp.bfloat16),
            pltpu.VMEM((devices * seg, width), jnp.bfloat16),
            pltpu.VMEM((width, latents), jnp.bfloat16),
            pltpu.VMEM((latents, width), jnp.bfloat16),
            pltpu.VMEM((groups, replicas, replicas * seg, latents), jnp.float32),
            pltpu.VMEM((devices * seg, latents), jnp.bfloat16),
            pltpu.VMEM((tok_rows, latents), jnp.bfloat16),
            pltpu.VMEM((8, width), jnp.float32),
            pltpu.VMEM((devices, 8, 128), jnp.float32),
            pltpu.VMEM((replicas * seg, width), jnp.bfloat16),
            pltpu.VMEM((latents, width), jnp.float32),
            dma((replicas + 2,)),
            dma((devices,)),
            dma((devices,)),
            dma((devices,)),
            dma((devices,)),
            dma((groups,)),
            dma((groups,)),
            dma((devices,)),
            dma((devices,)),
        ],
        compiler_params=pltpu.CompilerParams(
            collective_id=0, has_side_effects=True, vmem_limit_bytes=60 * 1024 * 1024
        ),
    )(
        block_ids.reshape(1, tok_rows),
        enc_bias,
        dec_bias.reshape(1, features),
        activations,
        enc_weight,
        dec_weight,
    )
    return loss[0, 0], codes, gradient


def spread(activations, block_ids, enc_weight, enc_bias, dec_weight, dec_bias):
    groups = lax.axis_size("latent")
    replicas = lax.axis_size("blk")
    tok_rows, features = activations.shape
    per_owner = tok_rows // groups
    block_of = block_ids[:, 0]
    matches = (block_of[:, None] == block_of[None, :]).astype(jnp.int32)
    earlier = jnp.sum(jnp.tril(matches, -1), axis=1)
    placed = block_of * per_owner + earlier
    source_row = (
        jnp.zeros((tok_rows,), jnp.int32).at[placed].set(jnp.arange(tok_rows, dtype=jnp.int32))
    )
    outgoing = activations[source_row]
    contract = (((0,), (0,)), ((), ()))
    incoming = lax.all_to_all(outgoing, "latent", split_axis=0, concat_axis=0, tiled=True)
    centered = (incoming.astype(jnp.float32) - dec_bias).astype(jnp.bfloat16)
    pre_codes = jnp.dot(centered, enc_weight[0], preferred_element_type=jnp.float32) + enc_bias[0]
    codes = jnp.maximum(pre_codes, 0.0).astype(jnp.bfloat16)
    error_rows = (
        jnp.dot(codes, dec_weight[0], preferred_element_type=jnp.float32)
        + dec_bias
        - incoming.astype(jnp.float32)
    )
    squares = jnp.sum(error_rows * error_rows)
    partial_grad = lax.dot_general(
        codes, error_rows.astype(jnp.bfloat16), contract, preferred_element_type=jnp.float32
    )
    summed = lax.psum_scatter(
        partial_grad.astype(jnp.bfloat16), "blk", scatter_dimension=1, tiled=True
    ).astype(jnp.float32)
    returned = lax.all_to_all(codes, "latent", split_axis=0, concat_axis=0, tiled=True)
    token_codes = returned[placed]
    gradient = summed / (tok_rows * replicas)
    summed_loss = lax.psum(squares, ("latent", "blk"))
    loss_value = summed_loss / (tok_rows * groups * replicas * features)
    return (loss_value, token_codes, gradient[None])


def solution(mesh):
    groups, replicas = mesh.shape["latent"], mesh.shape["blk"]
    placed = (
        P(("latent", "blk"), None),
        P(("latent", "blk"), None),
        P("latent", None, None),
        P("latent", None),
        P("latent", None, None),
        P(),
    )

    def local(activations, *rest):
        tok_rows, features = activations.shape
        fits = (
            groups & (groups - 1) == 0
            and replicas & (replicas - 1) == 0
            and 1 < groups <= tok_rows
            and tok_rows % (16 * groups) == 0
            and features % (128 * replicas) == 0
        )
        return (routed if fits else spread)(activations, *rest)

    return jax.shard_map(
        local,
        mesh=mesh,
        in_specs=placed,
        out_specs=(P(), P(("latent", "blk"), None), P("latent", None, "blk")),
        check_vma=False,
    )
```

time: 80 us -> 79.3 us (level)
  local copies, waits for them, and re-layouts: 8.53 us -> 3.67 us
  Pallas kernels: 68.8 us -> 72.9 us
    unnamed x13 -> x2, local copies, waits for them, and re-layouts: 8.53 us -> 3.67 us
    pallas_call x1, Pallas kernels: 68.8 us -> 72.9 us  [routed(): pl.pallas_call(functools.partial(kernel, groups, replicas, tile), out_sha...]
where the time goes in v2:
time: 79.3 us; the launch traced here: 79 us
  Pallas kernels  72.9 us (92%)
  local copies, waits for them, and re-layouts  3.67 us (5%)
  between operations  2.4 us (3%)
    pallas_call x1, Pallas kernels, routed(): pl.pallas_call(functools.partial(kernel, groups, replicas, tile), out_sha...  72.9 us
    unnamed x2, local copies, waits for them, and re-layouts  3.67 us

profile of v2, /device:TPU:0, one launch (start us, length us, event | category | flops | bytes accessed | tf_op | source)
XLA Modules:
  0.0 79.0 jit_solution(17529092687749606040)
XLA Ops:
  0.6 72.9 %shard_map.85 = (f32[1,1]{1,0:T(1,128)}, bf16[128,128]{1,0:T(8,128)(2,1)}, f32[1,128,2048]{2,1,0:T(8,128)}) custom-call(s32[1,128]{1,0:T(1,128)} %bitcast.4, f32[1,128]{1,0:T(1,128)} %enc_bias_ref.1, f32[1,8192]{1,0:T(1,128)} %bitcast.3, bf16[128,8192]{1,0:T(8,128)(2,1)} %act_hbm.1, bf16[1,8192,128]{2,1,0:T(8,128)(2,1)} %enc_hbm.1, bf16[1,128,8192]{2,1,0:T(8,128)(2,1)} %dec_hbm.1), custom_call_target="tpu_custom_call" | custom-call | tf_op jit(solution)/shard_map/pallas_call | solution.py:313
  74.2 1.4 %copy.13 = bf16[128,128]{1,0:T(8,128)(2,1)} copy(bf16[128,128]{1,0:T(8,128)(2,1)} %get-tuple-element.13) | data formatting | bytes 65536
  75.5 2.3 %copy.14 = f32[1,128,2048]{2,1,0:T(8,128)} copy(f32[1,128,2048]{2,1,0:T(8,128)} %get-tuple-element.14) | data formatting | bytes 2097152

commit v3 on v2

--- a/solution.py
+++ b/solution.py
@@ -24,15 +24,18 @@
     groups,
     replicas,
     tile,
-    ids_ref,
-    enc_bias_ref,
-    dec_bias_ref,
+    ids_hbm,
+    enc_bias_hbm,
+    dec_bias_hbm,
     act_hbm,
     enc_hbm,
     dec_hbm,
     loss_ref,
     codes_out_ref,
-    grad_hbm,
+    grad_ref,
+    ids_ref,
+    enc_bias_ref,
+    dec_bias_ref,
     act,
     ordered,
     arrived,
@@ -42,9 +45,9 @@
     codes,
     returned,
     squares,
+    level_losses,
     losses,
     error_low,
-    grad,
     load_sem,
     row_send,
     row_recv,
@@ -54,6 +57,8 @@
     code_recv,
     loss_send,
     loss_recv,
+    total_send,
+    total_recv,
 ):
     lat, blk = lax.axis_index("latent"), lax.axis_index("blk")
     tok_rows, features = act.shape
@@ -71,6 +76,8 @@
         return (flip(lat, j), flip(blk, e))
 
     barrier = pltpu.get_barrier_semaphore()
+    load_ids = pltpu.make_async_copy(ids_hbm, ids_ref, load_sem.at[replicas + 2])
+    load_ids.start()
     loads = []
     for e in range(replicas):
         cols = pl.ds(pl.multiple_of(flip(blk, e) * width, width), width)
@@ -83,12 +90,17 @@
     load_dec = pltpu.make_async_copy(
         dec_hbm.at[0, :, pl.ds(own_cols, width)], dec, load_sem.at[replicas + 1]
     )
+    load_biases = [
+        pltpu.make_async_copy(enc_bias_hbm, enc_bias_ref, load_sem.at[replicas + 3]),
+        pltpu.make_async_copy(dec_bias_hbm, dec_bias_ref, load_sem.at[replicas + 4]),
+    ]
     for load in loads:
         load.start()
-    for j, e in peers:
+    for j, e in reversed(peers):
         pl.semaphore_signal(barrier, inc=1, device_id=device(j, e), device_id_type=MESH)
-    load_enc.start()
-    load_dec.start()
+    for load in (load_enc, load_dec, *load_biases):
+        load.start()
+    load_ids.wait()
 
     ids = ids_ref[...]
     square = (tok_rows, tok_rows)
@@ -149,8 +161,12 @@
         for at in range(ahead):
             send_rows(at, e)
 
-    load_enc.wait()
-    load_dec.wait()
+    for at in range(ahead, groups):
+        for e in range(replicas):
+            send_rows(at, e)
+
+    for load in (load_enc, load_dec, *load_biases):
+        load.wait()
     squares[...] = jnp.zeros_like(squares)
     part_copies, code_copies = [], []
 
@@ -229,10 +245,10 @@
             cols = pl.ds(pl.multiple_of(i * tile, tile), tile)
             term = jnp.dot(flipped, error_low[:, cols], preferred_element_type=jnp.float32)
             if at > 0:
-                term = grad[:, cols] + term
+                term = grad_ref[0, :, cols] + term
             if at == groups - 1:
                 term = term / (tok_rows * replicas)
-            grad[:, cols] = term
+            grad_ref[0, :, cols] = term
             return carry
 
         lax.fori_loop(0, tiles, errors, 0)
@@ -240,37 +256,44 @@
             send_squares()
         lax.fori_loop(0, tiles, gradient, 0)
 
-    place_of = lat * replicas + blk
-    loss_copies = []
+    loss_copies, total_copies = [], []
 
     def send_squares():
         own = squares[:, :128]
         for i in range(1, width // 128):
             own = own + squares[:, i * 128 : (i + 1) * 128]
-        losses[place_of] = own
-        for j, e in peers:
+        level_losses[lat] = own
+        for j in range(groups - 1, 0, -1):
             copy = pltpu.make_async_remote_copy(
-                src_ref=losses.at[place_of],
-                dst_ref=losses.at[place_of],
-                send_sem=loss_send.at[j * replicas + e],
-                recv_sem=loss_recv.at[j * replicas + e],
-                device_id=device(j, e),
+                src_ref=level_losses.at[lat],
+                dst_ref=level_losses.at[lat],
+                send_sem=loss_send.at[j],
+                recv_sem=loss_recv.at[j],
+                device_id=device(j, 0),
                 device_id_type=MESH,
             )
             copy.start()
             loss_copies.append(copy)
 
     for at in range(groups):
-        if at + ahead < groups:
-            wait_sent(at)
-            for e in range(replicas):
-                send_rows(at + ahead, e)
         encode(at)
         if at > 0:
             decode(at - 1)
     decode(groups - 1)
-    store = pltpu.make_async_copy(grad, grad_hbm.at[0], load_sem.at[0])
-    store.start()
+    for copy in loss_copies:
+        copy.wait_recv()
+    losses[blk] = jnp.sum(level_losses[...], axis=0)
+    for e in range(replicas - 1, 0, -1):
+        copy = pltpu.make_async_remote_copy(
+            src_ref=losses.at[blk],
+            dst_ref=losses.at[blk],
+            send_sem=total_send.at[e],
+            recv_sem=total_recv.at[e],
+            device_id=device(0, e),
+            device_id_type=MESH,
+        )
+        copy.start()
+        total_copies.append(copy)
 
     for j, copy in code_copies:
         if j == 0:
@@ -281,17 +304,16 @@
         placed.T.astype(jnp.bfloat16), returned[...], preferred_element_type=jnp.float32
     ).astype(jnp.bfloat16)
 
-    for copy in loss_copies:
+    for copy in total_copies:
         copy.wait_recv()
     total = jnp.sum(losses[...], axis=0)
     loss_ref[...] = jnp.sum(total, keepdims=True) / (
         tok_rows * groups * replicas * features
     )
 
-    store.wait()
-    for at in range(groups - ahead, groups):
+    for at in range(groups):
         wait_sent(at)
-    for copy in part_copies + loss_copies:
+    for copy in part_copies + loss_copies + total_copies:
         copy.wait_send()
     for j, copy in code_copies:
         if j > 0:
@@ -308,7 +330,7 @@
     width = features // replicas
     tile = math.gcd(512, width)
     vmem = pl.BlockSpec(memory_space=pltpu.VMEM)
-    hbm = pl.BlockSpec(memory_space=pl.ANY)
+    hbm = pl.BlockSpec(memory_space=pltpu.HBM)
     dma = pltpu.SemaphoreType.DMA
     loss, codes, gradient = pl.pallas_call(
         functools.partial(kernel, groups, replicas, tile),
@@ -317,9 +339,12 @@
             jax.ShapeDtypeStruct((tok_rows, latents), jnp.bfloat16),
             jax.ShapeDtypeStruct((1, latents, width), jnp.float32),
         ),
-        in_specs=[vmem, vmem, vmem, hbm, hbm, hbm],
-        out_specs=(vmem, vmem, hbm),
+        in_specs=[hbm] * 6,
+        out_specs=(vmem, vmem, vmem),
         scratch_shapes=[
+            pltpu.VMEM((1, tok_rows), jnp.int32),
+            pltpu.VMEM((1, latents), jnp.float32),
+            pltpu.VMEM((1, features), jnp.float32),
             pltpu.VMEM((tok_rows, features), jnp.bfloat16),
             pltpu.VMEM((tok_rows, features), jnp.bfloat16),
             pltpu.VMEM((devices * seg, width), jnp.bfloat16),
@@ -329,21 +354,23 @@
             pltpu.VMEM((devices * seg, latents), jnp.bfloat16),
             pltpu.VMEM((tok_rows, latents), jnp.bfloat16),
             pltpu.VMEM((8, width), jnp.float32),
-            pltpu.VMEM((devices, 8, 128), jnp.float32),
+            pltpu.VMEM((groups, 8, 128), jnp.float32),
+            pltpu.VMEM((replicas, 8, 128), jnp.float32),
             pltpu.VMEM((replicas * seg, width), jnp.bfloat16),
-            pltpu.VMEM((latents, width), jnp.float32),
-            dma((replicas + 2,)),
+            dma((replicas + 5,)),
             dma((devices,)),
             dma((devices,)),
             dma((devices,)),
             dma((devices,)),
             dma((groups,)),
             dma((groups,)),
-            dma((devices,)),
-            dma((devices,)),
+            dma((groups,)),
+            dma((groups,)),
+            dma((replicas,)),
+            dma((replicas,)),
         ],
         compiler_params=pltpu.CompilerParams(
-            collective_id=0, has_side_effects=True, vmem_limit_bytes=60 * 1024 * 1024
+            collective_id=0, has_side_effects=True, vmem_limit_bytes=52 * 1024 * 1024
         ),
     )(
         block_ids.reshape(1, tok_rows),

time: 79.3 us -> 76.9 us (0.970)
  Pallas kernels: 72.9 us -> 70.7 us
    pallas_call x1, Pallas kernels: 72.9 us -> 70.7 us  [routed(): pl.pallas_call(functools.partial(kernel, groups, replicas, tile), out_sha...]
    unnamed x2 -> x8, local copies, waits for them, and re-layouts: 3.67 us -> 3.65 us
where the time goes in v3:
time: 76.9 us; the launch traced here: 76.7 us
  Pallas kernels  70.7 us (92%)
  local copies, waits for them, and re-layouts  3.65 us (5%)
  between operations  2.39 us (3%)
    pallas_call x1, Pallas kernels, routed(): pl.pallas_call(functools.partial(kernel, groups, replicas, tile), out_sha...  70.7 us
    unnamed x8, local copies, waits for them, and re-layouts  3.65 us

profile of v3, /device:TPU:0, one launch (start us, length us, event | category | flops | bytes accessed | tf_op | source)
XLA Modules:
  0.0 76.7 jit_solution(12541345261460632899)
XLA Ops:
  0.6 0.0 copy-start
  0.6 0.7 copy-done
  1.4 0.0 copy-start.1
  1.4 0.7 copy-done.1
  2.0 0.0 copy-start.2
  2.0 0.7 copy-done.2
  2.7 70.7 %shard_map.85 = (f32[1,1]{1,0:T(1,128)}, bf16[128,128]{1,0:T(8,128)(2,1)S(1)}, f32[1,128,2048]{2,1,0:T(8,128)S(1)}) custom-call(s32[1,128]{1,0:T(1,128)S(1)} %bitcast.4, f32[1,128]{1,0:T(1,128)S(1)} %copy-done.2, f32[1,8192]{1,0:T(1,128)S(1)} %bitcast.3, bf16[128,8192]{1,0:T(8,128)(2,1)} %act_hbm.1, bf16[1,8192,128]{2,1,0:T(8,128)(2,1)} %enc_hbm.1, ...), custom_call_target="tpu_custom_call" | custom-call | tf_op jit(solution)/shard_map/pallas_call | solution.py:335
  74.0 0.6 copy.13
  74.6 1.0 %copy.14 = f32[1,128,2048]{2,1,0:T(8,128)} copy(f32[1,128,2048]{2,1,0:T(8,128)S(1)} %get-tuple-element.14) | data formatting | bytes 2097152
Async XLA Ops:
  0.6 0.8 copy-start
  1.4 0.7 copy-start.1
  2.0 0.7 copy-start.2

commit v4 on v3

--- a/solution.py
+++ b/solution.py
@@ -38,6 +38,7 @@
     dec_bias_ref,
     act,
     ordered,
+    staged,
     arrived,
     enc,
     dec,
@@ -51,6 +52,8 @@
     load_sem,
     row_send,
     row_recv,
+    column_send,
+    column_recv,
     part_send,
     part_recv,
     code_send,
@@ -69,8 +72,7 @@
     group_rows = replicas * seg
     own_cols = pl.multiple_of(blk * width, width)
     order = [j for i in range(groups // 2) for j in (groups // 2 - 1 - i, groups // 2 + i)]
-    ahead = min(4, groups)
-    peers = [(j, e) for j in range(groups) for e in range(replicas) if (j, e) != (0, 0)]
+    peers = [(j, 0) for j in range(1, groups)] + [(0, e) for e in range(1, replicas)]
 
     def device(j, e):
         return (flip(lat, j), flip(blk, e))
@@ -116,17 +118,22 @@
     placed = (place == down.astype(jnp.float32)).astype(jnp.float32)
     to_place = placed.astype(jnp.bfloat16)
 
-    row_copies = {}
+    row_copies, column_copies = {}, {}
+
+    def piece(j, e):
+        return (
+            pl.ds(pl.multiple_of(flip(lat, j) * seg, seg), seg),
+            pl.ds(pl.multiple_of(flip(blk, e) * width, width), width),
+        )
+
+    def place_at(at, e):
+        return pl.ds(pl.multiple_of((at * replicas + flip(blk, e)) * seg, seg), seg)
 
     def send_rows(at, e):
         j = order[at]
-        owner, column = device(j, e)
-        source = ordered.at[
-            pl.ds(pl.multiple_of(owner * seg, seg), seg),
-            pl.ds(pl.multiple_of(column * width, width), width),
-        ]
-        target = arrived.at[pl.ds(pl.multiple_of((at * replicas + blk) * seg, seg), seg), :]
-        if (j, e) == (0, 0):
+        target = arrived.at[place_at(at, e), :]
+        source = ordered.at[piece(j, e)] if e == 0 else staged.at[place_at(at, e), :]
+        if j == 0:
             copy = pltpu.make_async_copy(source, target, row_recv.at[0])
         else:
             copy = pltpu.make_async_remote_copy(
@@ -134,16 +141,25 @@
                 dst_ref=target,
                 send_sem=row_send.at[j * replicas + e],
                 recv_sem=row_recv.at[j * replicas + e],
-                device_id=(owner, column),
+                device_id=device(j, 0),
                 device_id_type=MESH,
             )
         copy.start()
         row_copies[j, e] = copy
 
-    def wait_sent(at):
-        for e in range(replicas):
-            if (order[at], e) != (0, 0):
-                row_copies[order[at], e].wait_send()
+    def send_columns(at, e):
+        j = order[at]
+        landing = arrived if j == 0 else staged
+        copy = pltpu.make_async_remote_copy(
+            src_ref=ordered.at[piece(j, e)],
+            dst_ref=landing.at[place_at(at, 0), :],
+            send_sem=column_send.at[j * replicas + e],
+            recv_sem=column_recv.at[j * replicas + e],
+            device_id=device(0, e),
+            device_id_type=MESH,
+        )
+        copy.start()
+        column_copies[j, e] = copy
 
     for e in range(replicas):
         loads[e].wait()
@@ -158,12 +174,16 @@
         lax.fori_loop(0, tiles, order_rows, 0)
         if e == 0:
             pl.semaphore_wait(barrier, len(peers))
-        for at in range(ahead):
-            send_rows(at, e)
-
-    for at in range(ahead, groups):
-        for e in range(replicas):
-            send_rows(at, e)
+            for at in range(groups):
+                send_rows(at, 0)
+    for at in range(groups):
+        for e in range(1, replicas):
+            send_columns(at, e)
+    for at in range(groups):
+        if order[at] > 0:
+            for e in range(1, replicas):
+                column_copies[order[at], e].wait_recv()
+                send_rows(at, e)
 
     for load in (load_enc, load_dec, *load_biases):
         load.wait()
@@ -174,6 +194,8 @@
         for e in range(replicas):
             if (order[at], e) == (0, 0):
                 row_copies[0, 0].wait()
+            elif order[at] == 0:
+                column_copies[0, e].wait_recv()
             else:
                 row_copies[order[at], e].wait_recv()
 
@@ -311,8 +333,11 @@
         tok_rows * groups * replicas * features
     )
 
-    for at in range(groups):
-        wait_sent(at)
+    for (j, e), copy in row_copies.items():
+        if j > 0:
+            copy.wait_send()
+    for copy in column_copies.values():
+        copy.wait_send()
     for copy in part_copies + loss_copies + total_copies:
         copy.wait_send()
     for j, copy in code_copies:
@@ -348,6 +373,7 @@
             pltpu.VMEM((tok_rows, features), jnp.bfloat16),
             pltpu.VMEM((tok_rows, features), jnp.bfloat16),
             pltpu.VMEM((devices * seg, width), jnp.bfloat16),
+            pltpu.VMEM((devices * seg, width), jnp.bfloat16),
             pltpu.VMEM((width, latents), jnp.bfloat16),
             pltpu.VMEM((latents, width), jnp.bfloat16),
             pltpu.VMEM((groups, replicas, replicas * seg, latents), jnp.float32),
@@ -358,6 +384,8 @@
             pltpu.VMEM((replicas, 8, 128), jnp.float32),
             pltpu.VMEM((replicas * seg, width), jnp.bfloat16),
             dma((replicas + 5,)),
+            dma((devices,)),
+            dma((devices,)),
             dma((devices,)),
             dma((devices,)),
             dma((devices,)),

time: 76.9 us -> 76.5 us (level)
  no operation moved by 1% of the time
where the time goes in v4:
time: 76.5 us; the launch traced here: 76.3 us
  Pallas kernels  70.2 us (92%)
  local copies, waits for them, and re-layouts  3.65 us (5%)
  between operations  2.39 us (3%)
    pallas_call x1, Pallas kernels, routed(): pl.pallas_call(functools.partial(kernel, groups, replicas, tile), out_sha...  70.2 us
    unnamed x8, local copies, waits for them, and re-layouts  3.65 us

profile of v4, /device:TPU:0, one launch (start us, length us, event | category | flops | bytes accessed | tf_op | source)
XLA Modules:
  0.0 76.3 jit_solution(11099158759969983698)
XLA Ops:
  0.6 0.0 copy-start
  0.6 0.7 copy-done
  1.4 0.0 copy-start.1
  1.4 0.7 copy-done.1
  2.0 0.0 copy-start.2
  2.0 0.7 copy-done.2
  2.7 70.2 %shard_map.85 = (f32[1,1]{1,0:T(1,128)}, bf16[128,128]{1,0:T(8,128)(2,1)S(1)}, f32[1,128,2048]{2,1,0:T(8,128)S(1)}) custom-call(s32[1,128]{1,0:T(1,128)S(1)} %bitcast.4, f32[1,128]{1,0:T(1,128)S(1)} %copy-done.2, f32[1,8192]{1,0:T(1,128)S(1)} %bitcast.3, bf16[128,8192]{1,0:T(8,128)(2,1)} %act_hbm.1, bf16[1,8192,128]{2,1,0:T(8,128)(2,1)} %enc_hbm.1, ...), custom_call_target="tpu_custom_call" | custom-call | tf_op jit(solution)/shard_map/pallas_call | solution.py:360
  73.6 0.6 copy.13
  74.2 1.0 %copy.14 = f32[1,128,2048]{2,1,0:T(8,128)} copy(f32[1,128,2048]{2,1,0:T(8,128)S(1)} %get-tuple-element.14) | data formatting | bytes 2097152
Async XLA Ops:
  0.6 0.8 copy-start
  1.4 0.7 copy-start.1
  2.0 0.7 copy-start.2

commit v5 on v4

--- a/solution.py
+++ b/solution.py
@@ -24,18 +24,14 @@
     groups,
     replicas,
     tile,
-    ids_hbm,
-    enc_bias_hbm,
-    dec_bias_hbm,
+    small_hbm,
     act_hbm,
     enc_hbm,
     dec_hbm,
     loss_ref,
     codes_out_ref,
     grad_ref,
-    ids_ref,
-    enc_bias_ref,
-    dec_bias_ref,
+    small,
     act,
     ordered,
     staged,
@@ -71,15 +67,17 @@
     tiles = width // tile
     group_rows = replicas * seg
     own_cols = pl.multiple_of(blk * width, width)
+    bias_at = tok_rows + latents + own_cols
     order = [j for i in range(groups // 2) for j in (groups // 2 - 1 - i, groups // 2 + i)]
+    ahead, window, lag = min(2, groups), replicas + 2, 3
     peers = [(j, 0) for j in range(1, groups)] + [(0, e) for e in range(1, replicas)]
 
     def device(j, e):
         return (flip(lat, j), flip(blk, e))
 
     barrier = pltpu.get_barrier_semaphore()
-    load_ids = pltpu.make_async_copy(ids_hbm, ids_ref, load_sem.at[replicas + 2])
-    load_ids.start()
+    load_small = pltpu.make_async_copy(small_hbm, small, load_sem.at[replicas + 2])
+    load_small.start()
     loads = []
     for e in range(replicas):
         cols = pl.ds(pl.multiple_of(flip(blk, e) * width, width), width)
@@ -92,29 +90,25 @@
     load_dec = pltpu.make_async_copy(
         dec_hbm.at[0, :, pl.ds(own_cols, width)], dec, load_sem.at[replicas + 1]
     )
-    load_biases = [
-        pltpu.make_async_copy(enc_bias_hbm, enc_bias_ref, load_sem.at[replicas + 3]),
-        pltpu.make_async_copy(dec_bias_hbm, dec_bias_ref, load_sem.at[replicas + 4]),
-    ]
     for load in loads:
         load.start()
     for j, e in reversed(peers):
         pl.semaphore_signal(barrier, inc=1, device_id=device(j, e), device_id_type=MESH)
-    for load in (load_enc, load_dec, *load_biases):
-        load.start()
-    load_ids.wait()
-
-    ids = ids_ref[...]
+    load_enc.start()
+    load_dec.start()
+    load_small.wait()
+
+    ids = small[:, :tok_rows]
     square = (tok_rows, tok_rows)
     down = lax.broadcasted_iota(jnp.int32, square, 0)
     along = lax.broadcasted_iota(jnp.int32, square, 1)
-    named = (ids == down).astype(jnp.float32)
+    named = (ids == down.astype(jnp.float32)).astype(jnp.float32)
     earlier = jnp.dot(
         named.astype(jnp.bfloat16),
         (down < along).astype(jnp.float32).astype(jnp.bfloat16),
         preferred_element_type=jnp.float32,
     )
-    place = jnp.sum(named * earlier, axis=0, keepdims=True) + ids.astype(jnp.float32) * seg
+    place = jnp.sum(named * earlier, axis=0, keepdims=True) + ids * seg
     placed = (place == down.astype(jnp.float32)).astype(jnp.float32)
     to_place = placed.astype(jnp.bfloat16)
 
@@ -174,19 +168,13 @@
         lax.fori_loop(0, tiles, order_rows, 0)
         if e == 0:
             pl.semaphore_wait(barrier, len(peers))
-            for at in range(groups):
+            for at in range(ahead):
                 send_rows(at, 0)
     for at in range(groups):
         for e in range(1, replicas):
             send_columns(at, e)
-    for at in range(groups):
-        if order[at] > 0:
-            for e in range(1, replicas):
-                column_copies[order[at], e].wait_recv()
-                send_rows(at, e)
-
-    for load in (load_enc, load_dec, *load_biases):
-        load.wait()
+    load_enc.wait()
+    load_dec.wait()
     squares[...] = jnp.zeros_like(squares)
     part_copies, code_copies = [], []
 
@@ -201,7 +189,7 @@
 
         def step(i, total):
             cols = pl.ds(pl.multiple_of(i * tile, tile), tile)
-            bias = dec_bias_ref[:, pl.ds(pl.multiple_of(own_cols + i * tile, tile), tile)]
+            bias = small[:, pl.ds(pl.multiple_of(bias_at + i * tile, 128), tile)]
             rows = arrived[pl.ds(at * group_rows, group_rows), cols]
             centered = (rows.astype(jnp.float32) - bias).astype(jnp.bfloat16)
             return total + jnp.dot(centered, enc[cols, :], preferred_element_type=jnp.float32)
@@ -227,7 +215,7 @@
         total = parts[at, 0]
         for d in range(1, replicas):
             total = total + parts[at, d]
-        wide = jnp.maximum(total + enc_bias_ref[...], 0.0)
+        wide = jnp.maximum(total + small[:, tok_rows : tok_rows + latents], 0.0)
         low = wide.astype(jnp.bfloat16)
         flipped = low.astype(jnp.float32).T.astype(jnp.bfloat16)
         codes[pl.ds(at * group_rows, group_rows), :] = low
@@ -250,7 +238,7 @@
 
         def errors(i, carry):
             cols = pl.ds(pl.multiple_of(i * tile, tile), tile)
-            bias = dec_bias_ref[:, pl.ds(pl.multiple_of(own_cols + i * tile, tile), tile)]
+            bias = small[:, pl.ds(pl.multiple_of(bias_at + i * tile, 128), tile)]
             rows = arrived[pl.ds(at * group_rows, group_rows), cols]
             error = (
                 jnp.dot(low, dec[:, cols], preferred_element_type=jnp.float32)
@@ -297,10 +285,26 @@
             copy.start()
             loss_copies.append(copy)
 
-    for at in range(groups):
-        encode(at)
-        if at > 0:
-            decode(at - 1)
+    far, sent = [], set()
+    for at in range(groups + lag):
+        if at < groups:
+            for e in range(replicas):
+                j = order[at]
+                if j >= groups // 2:
+                    if len(far) >= window:
+                        row_copies[far[-window]].wait_send()
+                        sent.add(far[-window])
+                    far.append((j, e))
+                if e == 0:
+                    if at >= ahead:
+                        send_rows(at, 0)
+                elif j > 0:
+                    column_copies[j, e].wait_recv()
+                    send_rows(at, e)
+        if at >= lag:
+            encode(at - lag)
+            if at > lag:
+                decode(at - lag - 1)
     decode(groups - 1)
     for copy in loss_copies:
         copy.wait_recv()
@@ -334,7 +338,7 @@
     )
 
     for (j, e), copy in row_copies.items():
-        if j > 0:
+        if j > 0 and (j, e) not in sent:
             copy.wait_send()
     for copy in column_copies.values():
         copy.wait_send()
@@ -364,12 +368,10 @@
             jax.ShapeDtypeStruct((tok_rows, latents), jnp.bfloat16),
             jax.ShapeDtypeStruct((1, latents, width), jnp.float32),
         ),
-        in_specs=[hbm] * 6,
+        in_specs=[hbm] * 4,
         out_specs=(vmem, vmem, vmem),
         scratch_shapes=[
-            pltpu.VMEM((1, tok_rows), jnp.int32),
-            pltpu.VMEM((1, latents), jnp.float32),
-            pltpu.VMEM((1, features), jnp.float32),
+            pltpu.VMEM((1, tok_rows + latents + features), jnp.float32),
             pltpu.VMEM((tok_rows, features), jnp.bfloat16),
             pltpu.VMEM((tok_rows, features), jnp.bfloat16),
             pltpu.VMEM((devices * seg, width), jnp.bfloat16),
@@ -401,9 +403,9 @@
             collective_id=0, has_side_effects=True, vmem_limit_bytes=52 * 1024 * 1024
         ),
     )(
-        block_ids.reshape(1, tok_rows),
-        enc_bias,
-        dec_bias.reshape(1, features),
+        jnp.concatenate(
+            (block_ids[:, 0].astype(jnp.float32), enc_bias[0], dec_bias)
+        ).reshape(1, tok_rows + latents + features),
         activations,
         enc_weight,
         dec_weight,
@@ -466,7 +468,9 @@
             groups & (groups - 1) == 0
             and replicas & (replicas - 1) == 0
             and 1 < groups <= tok_rows
+            and tok_rows % 128 == 0
             and tok_rows % (16 * groups) == 0
+            and rest[1].shape[2] % 128 == 0
             and features % (128 * replicas) == 0
         )
         return (routed if fits else spread)(activations, *rest)

time: 76.5 us -> 80 us (1.046)
  Pallas kernels: 70.2 us -> 74.4 us
  local copies, waits for them, and re-layouts: 3.65 us -> 1.61 us
  other arithmetic: 0 us -> 1.43 us
    pallas_call x1, Pallas kernels: 70.2 us -> 74.4 us  [routed(): pl.pallas_call(functools.partial(kernel, groups, replicas, tile), out_sha...]
    unnamed x8 -> x2, local copies, waits for them, and re-layouts: 3.65 us -> 1.59 us
where the time goes in v5:
time: 80 us; the launch traced here: 79.8 us
  Pallas kernels  74.4 us (93%)
  between operations  2.33 us (3%)
  local copies, waits for them, and re-layouts  1.61 us (2%)
  other arithmetic  1.43 us (2%)
    pallas_call x1, Pallas kernels, routed(): pl.pallas_call(functools.partial(kernel, groups, replicas, tile), out_sha...  74.4 us

profile of v5, /device:TPU:0, one launch (start us, length us, event | category | flops | bytes accessed | tf_op | source)
XLA Modules:
  0.0 79.8 jit_solution(5317191402870011774)
XLA Ops:
  0.6 0.7 convert_bitcast_fusion
  1.3 0.8 pad_maximum_fusion
  2.1 74.4 %shard_map.85 = (f32[1,1]{1,0:T(1,128)}, bf16[128,128]{1,0:T(8,128)(2,1)S(1)}, f32[1,128,2048]{2,1,0:T(8,128)S(1)}) custom-call(f32[1,8448]{1,0:T(1,128)S(1)} %reshape.10.small_hbm, bf16[128,8192]{1,0:T(8,128)(2,1)} %act_hbm.1, bf16[1,8192,128]{2,1,0:T(8,128)(2,1)} %enc_hbm.1, bf16[1,128,8192]{2,1,0:T(8,128)(2,1)} %dec_hbm.1), custom_call_target="tpu_custom_call" | custom-call | tf_op jit(solution)/shard_map/pallas_call | solution.py:364
  77.1 0.6 copy.13
  77.7 1.0 %copy.14 = f32[1,128,2048]{2,1,0:T(8,128)} copy(f32[1,128,2048]{2,1,0:T(8,128)S(1)} %get-tuple-element.14) | data formatting | bytes 2097152
  (1 shorter events, 0.0 us)

commit v6 on v5

--- a/solution.py
+++ b/solution.py
@@ -68,8 +68,8 @@
     group_rows = replicas * seg
     own_cols = pl.multiple_of(blk * width, width)
     bias_at = tok_rows + latents + own_cols
-    order = [j for i in range(groups // 2) for j in (groups // 2 - 1 - i, groups // 2 + i)]
-    ahead, window, lag = min(2, groups), replicas + 2, 3
+    order = list(range(groups // 2 - 1, -1, -1)) + list(range(groups // 2, groups))
+    turns = [at for i in range(groups // 2) for at in (groups // 2 + i, i)]
     peers = [(j, 0) for j in range(1, groups)] + [(0, e) for e in range(1, replicas)]
 
     def device(j, e):
@@ -165,14 +165,20 @@
             ).astype(jnp.bfloat16)
             return carry
 
-        lax.fori_loop(0, tiles, order_rows, 0)
+        lax.fori_loop(0, tiles, order_rows, 0, unroll=True)
         if e == 0:
             pl.semaphore_wait(barrier, len(peers))
-            for at in range(ahead):
+            for at in turns:
                 send_rows(at, 0)
-    for at in range(groups):
+    for at in turns:
         for e in range(1, replicas):
             send_columns(at, e)
+    for at in turns:
+        if order[at] > 0:
+            for e in range(1, replicas):
+                column_copies[order[at], e].wait_recv()
+                send_rows(at, e)
+
     load_enc.wait()
     load_dec.wait()
     squares[...] = jnp.zeros_like(squares)
@@ -195,7 +201,7 @@
             return total + jnp.dot(centered, enc[cols, :], preferred_element_type=jnp.float32)
 
         parts[at, blk] = lax.fori_loop(
-            0, tiles, step, jnp.zeros((group_rows, latents), jnp.float32)
+            0, tiles, step, jnp.zeros((group_rows, latents), jnp.float32), unroll=True
         )
         for e in range(1, replicas):
             copy = pltpu.make_async_remote_copy(
@@ -261,10 +267,10 @@
             grad_ref[0, :, cols] = term
             return carry
 
-        lax.fori_loop(0, tiles, errors, 0)
+        lax.fori_loop(0, tiles, errors, 0, unroll=True)
         if at == groups - 1:
             send_squares()
-        lax.fori_loop(0, tiles, gradient, 0)
+        lax.fori_loop(0, tiles, gradient, 0, unroll=True)
 
     loss_copies, total_copies = [], []
 
@@ -285,26 +291,10 @@
             copy.start()
             loss_copies.append(copy)
 
-    far, sent = [], set()
-    for at in range(groups + lag):
-        if at < groups:
-            for e in range(replicas):
-                j = order[at]
-                if j >= groups // 2:
-                    if len(far) >= window:
-                        row_copies[far[-window]].wait_send()
-                        sent.add(far[-window])
-                    far.append((j, e))
-                if e == 0:
-                    if at >= ahead:
-                        send_rows(at, 0)
-                elif j > 0:
-                    column_copies[j, e].wait_recv()
-                    send_rows(at, e)
-        if at >= lag:
-            encode(at - lag)
-            if at > lag:
-                decode(at - lag - 1)
+    for at in range(groups):
+        encode(at)
+        if at > 0:
+            decode(at - 1)
     decode(groups - 1)
     for copy in loss_copies:
         copy.wait_recv()
@@ -338,7 +328,7 @@
     )
 
     for (j, e), copy in row_copies.items():
-        if j > 0 and (j, e) not in sent:
+        if j > 0:
             copy.wait_send()
     for copy in column_copies.values():
         copy.wait_send()

time: 80 us -> 71.1 us (0.89)
  Pallas kernels: 74.4 us -> 65.5 us
    pallas_call x1, Pallas kernels: 74.4 us -> 65.5 us  [routed(): pl.pallas_call(functools.partial(kernel, groups, replicas, tile), out_sha...]
where the time goes in v6:
time: 71.1 us; the launch traced here: 70.9 us
  Pallas kernels  65.5 us (92%)
  between operations  2.33 us (3%)
  local copies, waits for them, and re-layouts  1.61 us (2%)
  other arithmetic  1.43 us (2%)
    pallas_call x1, Pallas kernels, routed(): pl.pallas_call(functools.partial(kernel, groups, replicas, tile), out_sha...  65.5 us
    unnamed x2, local copies, waits for them, and re-layouts  1.59 us

profile of v6, /device:TPU:0, one launch (start us, length us, event | category | flops | bytes accessed | tf_op | source)
XLA Modules:
  0.0 70.9 jit_solution(6558764446023025548)
XLA Ops:
  0.6 0.7 convert_bitcast_fusion
  1.3 0.8 %pad_maximum_fusion = f32[8448]{0:T(1024)S(1)} fusion(f32[8192]{0:T(1024)} %param.11, f32[128]{0:T(128)} %bitcast.4, f32[128]{0:T(128)S(1)} %convert_bitcast_fusion), kind=kLoop, calls=%fused_computation | loop fusion | flops 16896 | bytes 67584 | tf_op jit(solution)/shard_map/concatenate | solution.py:396
  2.1 65.5 %shard_map.85 = (f32[1,1]{1,0:T(1,128)}, bf16[128,128]{1,0:T(8,128)(2,1)S(1)}, f32[1,128,2048]{2,1,0:T(8,128)S(1)}) custom-call(f32[1,8448]{1,0:T(1,128)S(1)} %reshape.10.small_hbm, bf16[128,8192]{1,0:T(8,128)(2,1)} %act_hbm.1, bf16[1,8192,128]{2,1,0:T(8,128)(2,1)} %enc_hbm.1, bf16[1,128,8192]{2,1,0:T(8,128)(2,1)} %dec_hbm.1), custom_call_target="tpu_custom_call" | custom-call | tf_op jit(solution)/shard_map/pallas_call | solution.py:354
  68.1 0.6 copy.13
  68.8 1.0 %copy.14 = f32[1,128,2048]{2,1,0:T(8,128)} copy(f32[1,128,2048]{2,1,0:T(8,128)S(1)} %get-tuple-element.14) | data formatting | bytes 2097152
  (1 shorter events, 0.0 us)

commit v7 on v6

--- a/solution.py
+++ b/solution.py
@@ -223,7 +223,6 @@
             total = total + parts[at, d]
         wide = jnp.maximum(total + small[:, tok_rows : tok_rows + latents], 0.0)
         low = wide.astype(jnp.bfloat16)
-        flipped = low.astype(jnp.float32).T.astype(jnp.bfloat16)
         codes[pl.ds(at * group_rows, group_rows), :] = low
         j = order[at]
         home = pl.ds(pl.multiple_of(lat * seg, seg), seg)
@@ -254,23 +253,12 @@
             squares[:, cols] += jnp.sum(
                 (error * error).reshape(group_rows // 8, 8, tile), axis=0
             )
-            error_low[:, cols] = error.astype(jnp.bfloat16)
-            return carry
-
-        def gradient(i, carry):
-            cols = pl.ds(pl.multiple_of(i * tile, tile), tile)
-            term = jnp.dot(flipped, error_low[:, cols], preferred_element_type=jnp.float32)
-            if at > 0:
-                term = grad_ref[0, :, cols] + term
-            if at == groups - 1:
-                term = term / (tok_rows * replicas)
-            grad_ref[0, :, cols] = term
+            error_low[pl.ds(at * group_rows, group_rows), cols] = error.astype(jnp.bfloat16)
             return carry
 
         lax.fori_loop(0, tiles, errors, 0, unroll=True)
         if at == groups - 1:
             send_squares()
-        lax.fori_loop(0, tiles, gradient, 0, unroll=True)
 
     loss_copies, total_copies = [], []
 
@@ -296,6 +284,16 @@
         if at > 0:
             decode(at - 1)
     decode(groups - 1)
+
+    flipped = codes[...].astype(jnp.float32).T.astype(jnp.bfloat16)
+
+    def gradient(i, carry):
+        cols = pl.ds(pl.multiple_of(i * tile, tile), tile)
+        term = jnp.dot(flipped, error_low[:, cols], preferred_element_type=jnp.float32)
+        grad_ref[0, :, cols] = term / (tok_rows * replicas)
+        return carry
+
+    lax.fori_loop(0, tiles // 2, gradient, 0, unroll=True)
     for copy in loss_copies:
         copy.wait_recv()
     losses[blk] = jnp.sum(level_losses[...], axis=0)
@@ -310,6 +308,7 @@
         )
         copy.start()
         total_copies.append(copy)
+    lax.fori_loop(tiles // 2, tiles, gradient, 0, unroll=True)
 
     for j, copy in code_copies:
         if j == 0:
@@ -374,7 +373,7 @@
             pltpu.VMEM((8, width), jnp.float32),
             pltpu.VMEM((groups, 8, 128), jnp.float32),
             pltpu.VMEM((replicas, 8, 128), jnp.float32),
-            pltpu.VMEM((replicas * seg, width), jnp.bfloat16),
+            pltpu.VMEM((devices * seg, width), jnp.bfloat16),
             dma((replicas + 5,)),
             dma((devices,)),
             dma((devices,)),

time: 71.1 us -> 71.1 us (level)
  no operation moved by 1% of the time
where the time goes in v7:
time: 71.1 us; the launch traced here: 70.9 us
  Pallas kernels  65.5 us (92%)
  between operations  2.33 us (3%)
  local copies, waits for them, and re-layouts  1.61 us (2%)
  other arithmetic  1.43 us (2%)
    pallas_call x1, Pallas kernels, routed(): pl.pallas_call(functools.partial(kernel, groups, replicas, tile), out_sha...  65.5 us
    unnamed x2, local copies, waits for them, and re-layouts  1.59 us

profile of v7, /device:TPU:0, one launch (start us, length us, event | category | flops | bytes accessed | tf_op | source)
XLA Modules:
  0.0 70.9 jit_solution(18076111099215503860)
XLA Ops:
  0.6 0.7 convert_bitcast_fusion
  1.3 0.8 %pad_maximum_fusion = f32[8448]{0:T(1024)S(1)} fusion(f32[8192]{0:T(1024)} %param.11, f32[128]{0:T(128)} %bitcast.4, f32[128]{0:T(128)S(1)} %convert_bitcast_fusion), kind=kLoop, calls=%fused_computation | loop fusion | flops 16896 | bytes 67584 | tf_op jit(solution)/shard_map/concatenate | solution.py:395
  2.1 65.5 %shard_map.85 = (f32[1,1]{1,0:T(1,128)}, bf16[128,128]{1,0:T(8,128)(2,1)S(1)}, f32[1,128,2048]{2,1,0:T(8,128)S(1)}) custom-call(f32[1,8448]{1,0:T(1,128)S(1)} %reshape.10.small_hbm, bf16[128,8192]{1,0:T(8,128)(2,1)} %act_hbm.1, bf16[1,8192,128]{2,1,0:T(8,128)(2,1)} %enc_hbm.1, bf16[1,128,8192]{2,1,0:T(8,128)(2,1)} %dec_hbm.1), custom_call_target="tpu_custom_call" | custom-call | tf_op jit(solution)/shard_map/pallas_call | solution.py:353
  68.1 0.6 copy.13
  68.8 1.0 %copy.14 = f32[1,128,2048]{2,1,0:T(8,128)} copy(f32[1,128,2048]{2,1,0:T(8,128)S(1)} %get-tuple-element.14) | data formatting | bytes 2097152
  (1 shorter events, 0.0 us)
